TPU v7x, 32 devices: a whole 2x2x4 slice. The times are simulated.
32 devices in a mesh: grp: 2 (over y), bond: 4 (over z), ops: 4 (over x, core).
Axes of the slice: x: 2, y: 2, z: 4, core: 2. Of those that a mesh axis runs over, the one named last changes fastest.
Arguments:
- wavefunction: bfloat16 [16, 16, 128, 128], P(('grp', 'bond'), 'ops'), parts along dimension 0, may hold values from -6 to 6
- left_blocks: bfloat16 [64, 8, 128, 128], P(('grp', 'ops'), 'bond'), parts along dimension 0, may hold values from -0.5 to 0.5
- right_blocks: bfloat16 [64, 8, 128, 128], P(('grp', 'ops'), 'bond'), parts along dimension 0, may hold values from -0.5 to 0.5
- site_blocks: float32 [64, 16, 16], P(('grp', 'ops')), parts along dimension 0, may hold values from -0.4375 to 0.4375
- preconditioner: float32 [16, 16, 128, 128], P(('grp', 'bond'), 'ops'), parts along dimension 0, may hold values from 0.5 to 4
- left_lengths: int32 [16], P(('grp', 'bond')), parts along dimension 0, may hold values from 1 to 128, 768 in all
- right_lengths: int32 [16], P(('grp', 'bond')), parts along dimension 0, may hold values from 1 to 128, 768 in all
- term_shift: int32 [64], P(('grp', 'ops')), parts along dimension 0, may hold values from -1 to 1
Outputs:
- first_sigma: float32 [16, 16, 128, 128], P(('grp', 'bond'), 'ops'), parts along dimension 0
- second_sigma: float32 [16, 16, 128, 128], P(('grp', 'bond'), 'ops'), parts along dimension 0
There are 2 independent parts, one for each index of `grp`. A program takes and returns all parts, laid end to end along the dimension named above; each array names one. Nothing has to cross between parts.
Inputs may be any that keep to these rules, and one draw needn't show every extreme that they name: `left_lengths`: the lengths of one array sum to 8 * (96) and the largest is exactly 128. `right_lengths`: the lengths of one array sum to 8 * (96) and the largest is exactly 128.
All inputs are finite; a program needn't handle non-finite values. No bound on the sum of `left_lengths` or of `right_lengths` on one device may be relied on, other than what follows from the above.
Results may differ from a plain program's by a relative error of at most 0.018.
Values may be sent and summed in bfloat16 or wider, within the bound.
A program may use at most 64 MiB of HBM per device.

v0:
```python
import jax
import jax.numpy as jnp
from jax import lax
from jax.sharding import PartitionSpec as P


def shifted(array, axis, by):
    count = lax.axis_size(axis)
    pairs = [(i, i + by) for i in range(count) if 0 <= i + by < count]
    return lax.ppermute(array, axis, pairs)


def valid_mask(left_lengths, right_lengths, width):
    offsets = jnp.arange(width, dtype=jnp.int32)
    row_valid = (offsets[None, :] < left_lengths[:, None]).astype(jnp.float32)
    col_valid = (offsets[None, :] < right_lengths[:, None]).astype(jnp.float32)
    return row_valid[:, None, :, None] * col_valid[:, None, None, :]


def apply_hamiltonian(local_vec, left_blocks, right_blocks, site_blocks, term_shift, valid):
    gathered = lax.all_gather(local_vec, "ops", axis=1, tiled=True)
    sectors = gathered.shape[0]
    states = gathered.shape[1]
    width = gathered.shape[2]

    def term_step(running, pieces):
        left_piece, right_piece, site_piece, shift_value = pieces
        right_done = jnp.einsum(
            "spac,sdc->spad", gathered, right_piece, preferred_element_type=jnp.float32
        ).astype(jnp.bfloat16)
        applied = jnp.einsum(
            "sab,spbd->spad", left_piece, right_done, preferred_element_type=jnp.float32
        )
        blended = jnp.einsum("qp,spad->sqad", site_piece, applied, precision=lax.Precision.HIGHEST)
        bucket_slot = shift_value + 1
        current = lax.dynamic_index_in_dim(running, bucket_slot, 0, keepdims=False)
        return (lax.dynamic_update_index_in_dim(running, current + blended, bucket_slot, 0), None)

    running, _ = lax.scan(
        term_step,
        jnp.zeros((3, sectors, states, width, width), jnp.float32),
        (left_blocks, right_blocks, site_blocks, term_shift),
    )
    rounded = running.astype(jnp.bfloat16)
    summed = lax.psum_scatter(
        rounded.astype(jnp.float32).astype(jnp.bfloat16), "ops", scatter_dimension=2, tiled=True
    ).astype(jnp.float32)
    falling = summed[0]
    staying = summed[1]
    rising = summed[2]
    moved_rise = jnp.concatenate(
        [
            shifted(rising[sectors - 1 :].astype(jnp.bfloat16), "bond", 1).astype(jnp.float32),
            rising[: sectors - 1],
        ],
        axis=0,
    )
    moved_fall = jnp.concatenate(
        [falling[1:], shifted(falling[:1].astype(jnp.bfloat16), "bond", -1).astype(jnp.float32)],
        axis=0,
    )
    result = staying + moved_rise + moved_fall
    return result * valid


def body(
    wavefunction,
    left_blocks,
    right_blocks,
    site_blocks,
    preconditioner,
    left_lengths,
    right_lengths,
    term_shift,
):
    valid = valid_mask(left_lengths, right_lengths, wavefunction.shape[2])
    start = wavefunction * valid.astype(jnp.bfloat16)
    first_sigma = apply_hamiltonian(
        start, left_blocks, right_blocks, site_blocks, term_shift, valid
    )
    wide_wave = start.astype(jnp.float32)
    wave_norm, wave_sigma = lax.psum(
        (jnp.sum(wide_wave * wide_wave), jnp.sum(wide_wave * first_sigma)), ("bond", "ops")
    )
    ritz_value = wave_sigma / wave_norm
    correction = (first_sigma - ritz_value * wide_wave) / preconditioner
    corr_norm = lax.psum(jnp.sum(correction * correction), ("bond", "ops"))
    next_vector = (correction * jnp.sqrt(wave_norm / (corr_norm + 1e-06))).astype(jnp.bfloat16)
    second_sigma = apply_hamiltonian(
        next_vector, left_blocks, right_blocks, site_blocks, term_shift, valid
    )
    return (first_sigma, second_sigma)


def solution(mesh):
    in_specs = (
        P(("grp", "bond"), "ops", None, None),
        P(("grp", "ops"), "bond", None, None),
        P(("grp", "ops"), "bond", None, None),
        P(("grp", "ops"), None, None),
        P(("grp", "bond"), "ops", None, None),
        P(("grp", "bond")),
        P(("grp", "bond")),
        P(("grp", "ops")),
    )
    out_specs = (P(("grp", "bond"), "ops", None, None), P(("grp", "bond"), "ops", None, None))
    return jax.shard_map(body, mesh=mesh, in_specs=in_specs, out_specs=out_specs, check_vma=False)
```

profile of v0, /device:TPU:1, one launch (start us, length us, event | category | flops | bytes accessed | tf_op | source)
XLA Modules:
  0.0 546.0 jit_solution(14463096614077247215)
XLA Ops:
  9.8 19.5 %all-gather.3.cloned.1.call-done = bf16[2,16,128,128]{3,2,1,0:T(8,128)(2,1)} async-done(((bf16[2,4,128,128]{3,2,1,0:T(8,128)(2,1)}), bf16[2,16,128,128]{3,2,1,0:T(8,128)(2,1)}) %all-gather.3.cloned.1.call-update) | async-done | bytes 1048592 | tf_op jit(solution)/shard_map/all_gather | solution.py:21
  29.4 3.4 broadcast.43.clone2
  32.8 128.1 %while.24 = (s32[]{:T(128)}, f32[3,2,16,128,128]{4,3,2,1,0:T(8,128)}, s32[8]{0:T(128)S(1)}, bf16[8,2,128,128]{3,2,1,0:T(8,128)(2,1)}, bf16[2,16,128,128]{3,2,1,0...) while((s32[]{:T(128)}, ...), condition=%wide.region_1.2_spmd, body=%wide.region_0.1_spmd.sunk | while | flops 369623040 | bytes 24256708 | solution.py:39
  36.0 2.9 fusion.77
  38.9 2.5 copy.68
  43.2 3.7 fusion.78
  52.0 2.9 fusion.77
  54.9 2.5 copy.68
  59.2 3.7 fusion.78
  68.0 2.9 fusion.77
  70.9 2.5 copy.68
  75.2 3.7 fusion.78
  84.0 2.9 fusion.77
  86.9 2.5 copy.68
  91.2 3.7 fusion.78
  94.9 2.0 copy_dynamic-update-slice_fusion.4
  100.0 2.9 fusion.77
  102.9 2.5 copy.68
  107.2 3.7 fusion.78
  116.1 2.9 fusion.77
  119.0 2.5 copy.68
  123.2 3.7 fusion.78
  132.1 2.9 fusion.77
  135.0 2.5 copy.68
  139.2 3.7 fusion.78
  148.1 2.9 fusion.77
  151.0 2.5 copy.68
  155.2 3.7 fusion.78
  160.9 5.2 convert_element_type.125
  168.0 66.2 %all-reduce.6.cloned.1.call-done = bf16[3,2,16,128,128]{4,3,2,1,0:T(8,128)(2,1)} async-done(((bf16[3,2,16,128,128]{4,3,2,1,0:T(8,128)(2,1)}), bf16[3,2,16,128,128]{4,3,2,1,0:T(8,128)(2,1)}) %all-reduce.6.cloned.1.call-update) | async-done | bytes 3145744
  235.2 3.1 collective-permute-start
  241.2 3.0 collective-permute-done.1
  245.1 31.7 %all-reduce.2 = (f32[]{:T(128)}, f32[]{:T(128)}) all-reduce(f32[]{:T(128)} %get-tuple-element.183, f32[]{:T(128)} %get-tuple-element.182), channel_id=1, replica_groups=mesh['grp'=2,'bond'=4,'ops'=4] {'bond','ops'}, use_global_device_ids=true, to_apply=%region_6.7 | all-reduce | flops 2 | bytes 16 | tf_op jit(solution)/shard_map/psum | solution.py:82
  278.8 30.1 %psum.23 = f32[]{:T(128)} all-reduce(f32[]{:T(128)} %multiply_reduce_fusion), channel_id=1, replica_groups=mesh['grp'=2,'bond'=4,'ops'=4] {'bond','ops'}, use_global_device_ids=true, to_apply=%region_8.9 | all-reduce | flops 1 | bytes 8 | tf_op jit(solution)/shard_map/psum | solution.py:87
  311.3 14.3 %all-gather.5.cloned.1.call-done = bf16[2,16,128,128]{3,2,1,0:T(8,128)(2,1)} async-done(((bf16[2,4,128,128]{3,2,1,0:T(8,128)(2,1)}), bf16[2,16,128,128]{3,2,1,0:T(8,128)(2,1)}) %all-gather.5.cloned.1.call-update) | async-done | bytes 1048592 | tf_op jit(solution)/shard_map/all_gather | solution.py:21
  325.5 3.4 broadcast.43.clone
  329.0 128.1 %while.25 = (s32[]{:T(128)}, f32[3,2,16,128,128]{4,3,2,1,0:T(8,128)}, s32[8]{0:T(128)S(1)}, bf16[8,2,128,128]{3,2,1,0:T(8,128)(2,1)}, bf16[2,16,128,128]{3,2,1,0...) while((s32[]{:T(128)}, ...), condition=%wide.region_10.11_spmd, body=%wide.region_9.10_spmd.sunk | while | flops 369623040 | bytes 24256708 | solution.py:39
  332.1 2.9 fusion.86
  335.0 2.5 copy.72
  339.3 3.7 fusion.87
  348.1 2.9 fusion.86
  351.1 2.5 copy.72
  355.3 3.7 fusion.87
  364.2 2.9 fusion.86
  367.1 2.5 copy.72
  371.3 3.7 fusion.87
  380.2 2.9 fusion.86
  383.1 2.5 copy.72
  387.3 3.7 fusion.87
  396.2 2.9 fusion.86
  399.1 2.5 copy.72
  403.4 3.7 fusion.87
  412.2 2.9 fusion.86
  415.1 2.5 copy.72
  419.4 3.7 fusion.87
  428.2 2.9 fusion.86
  431.1 2.5 copy.72
  435.4 3.7 fusion.87
  444.2 2.9 fusion.86
  447.1 2.5 copy.72
  451.4 3.7 fusion.87
  457.1 5.2 convert_element_type.133
  462.3 68.1 %all-reduce.8.cloned.1.call-done = bf16[3,2,16,128,128]{4,3,2,1,0:T(8,128)(2,1)} async-done(((bf16[3,2,16,128,128]{4,3,2,1,0:T(8,128)(2,1)}), bf16[3,2,16,128,128]{4,3,2,1,0:T(8,128)(2,1)}) %all-reduce.8.cloned.1.call-update) | async-done | bytes 3145744
  532.6 4.0 collective-permute-start.2
  (108 shorter events, 102.3 us)
Async XLA Ops:
  7.2 22.2 %all-gather.3.cloned.1.call-start = ((), (), s32[]{:S(2)}) async-start(), calls=%async_computation | async-start | bytes 1310720 | tf_op jit(solution)/shard_map/all_gather | solution.py:21
  9.8 224.4 %all-reduce.6.cloned.1.call-start = ((), (), s32[]{:S(2)}) async-start(), calls=%async_computation.2 | async-start | bytes 6291456
  9.8 23.0 %copy-start.5 = (s32[8]{0:T(128)S(1)}, s32[8]{0:T(128)}, u32[]{:S(2)}) copy-start(s32[8]{0:T(128)} %param.19) | copy-start | bytes 100
  29.4 3.4 copy-start.1
  166.1 0.7 copy-start.6
  166.1 159.4 %all-gather.5.cloned.1.call-start = ((), (), s32[]{:S(2)}) async-start(), calls=%async_computation.1 | async-start | bytes 1310720 | tf_op jit(solution)/shard_map/all_gather | solution.py:21
  235.2 5.9 %collective-permute-start = (bf16[1,4,128,128]{3,2,1,0:T(8,128)(2,1)S(1)}, bf16[1,4,128,128]{3,2,1,0:T(8,128)(2,1)S(1)}, u32[]{:S(2)}, u32[]{:S(2)}) collective-permute-start(bf16[1,4,128,128]{3,2,1,0:T(8,128)(2,1)S(1)} %get-tuple-element.217), channel_id=1, source_target_pairs={{0,4},{4,8},{8,12},{1,5},{5,9},{9,13},{2,6},{6,10},{10,14},{3,7},{... | collective-permute-start | bytes 393224 | tf_op jit(solution)/shard_map/ppermute | solution.py:10
  238.3 5.9 %copy-start.3 = (bf16[2,4,128,128]{3,2,1,0:T(8,128)(2,1)S(1)}, bf16[2,4,128,128]{3,2,1,0:T(8,128)(2,1)}, u32[]{:S(2)}) copy-start(bf16[2,4,128,128]{3,2,1,0:T(8,128)(2,1)} %param.12) | copy-start | bytes 786436
  238.3 5.8 %collective-permute-start.1 = (bf16[1,4,128,128]{3,2,1,0:T(8,128)(2,1)S(1)}, bf16[1,4,128,128]{3,2,1,0:T(8,128)(2,1)S(1)}, u32[]{:S(2)}, u32[]{:S(2)}) collective-permute-start(bf16[1,4,128,128]{3,2,1,0:T(8,128)(2,1)S(1)} %get-tuple-element.218), channel_id=1, source_target_pairs={{4,0},{8,4},{12,8},{5,1},{9,5},{13,9},{6,2},{10,6},{14,10},{7,3},{... | collective-permute-start | bytes 393224 | tf_op jit(solution)/shard_map/ppermute | solution.py:10
  241.1 37.0 %copy-start.4 = (f32[2,4,128,128]{3,2,1,0:T(8,128)S(1)}, f32[2,4,128,128]{3,2,1,0:T(8,128)}, u32[]{:S(2)}) copy-start(f32[2,4,128,128]{3,2,1,0:T(8,128)} %param.16) | copy-start | bytes 1572868
  245.1 83.9 %copy-start.2 = (f32[2,4,128,128]{3,2,1,0:T(8,128)}, f32[2,4,128,128]{3,2,1,0:T(8,128)S(1)}, u32[]{:S(2)}) copy-start(f32[2,4,128,128]{3,2,1,0:T(8,128)S(1)} %get-tuple-element.214) | copy-start | bytes 1572868
  311.0 219.3 %all-reduce.8.cloned.1.call-start = ((), (), s32[]{:S(2)}) async-start(), calls=%async_computation.3 | async-start | bytes 6291456
  325.5 3.4 copy-start
  531.3 6.7 %collective-permute-start.3 = (bf16[1,4,128,128]{3,2,1,0:T(8,128)(2,1)S(1)}, bf16[1,4,128,128]{3,2,1,0:T(8,128)(2,1)S(1)}, u32[]{:S(2)}, u32[]{:S(2)}) collective-permute-start(bf16[1,4,128,128]{3,2,1,0:T(8,128)(2,1)S(1)} %get-tuple-element.215), channel_id=1, source_target_pairs={{4,0},{8,4},{12,8},{5,1},{9,5},{13,9},{6,2},{10,6},{14,10},{7,3},{... | collective-permute-start | bytes 393224 | tf_op jit(solution)/shard_map/ppermute | solution.py:10
  532.6 5.9 %collective-permute-start.2 = (bf16[1,4,128,128]{3,2,1,0:T(8,128)(2,1)S(1)}, bf16[1,4,128,128]{3,2,1,0:T(8,128)(2,1)S(1)}, u32[]{:S(2)}, u32[]{:S(2)}) collective-permute-start(bf16[1,4,128,128]{3,2,1,0:T(8,128)(2,1)S(1)} %get-tuple-element.216), channel_id=1, source_target_pairs={{0,4},{4,8},{8,12},{1,5},{5,9},{9,13},{2,6},{6,10},{10,14},{3,7},{... | collective-permute-start | bytes 393224 | tf_op jit(solution)/shard_map/ppermute | solution.py:10
Sparse Core Ops, SparseCore 0:
  10.1 19.1 all-gather.2
  166.2 67.9 all-reduce.5
  311.2 14.3 all-gather.4
  462.4 67.9 all-reduce.7
where the time goes:
time: 552 us; the launch traced here: 546 us
  waiting for transfers between devices  172 us (31%)
  matrix products  126 us (23%)
  local copies, waits for them, and re-layouts  119 us (22%)
  blocking collectives  61.8 us (11%)
  loops' own time  21.3 us (4%)
  other arithmetic  19 us (3%)
  between operations  17.1 us (3%)
  starting transfers between devices  10.2 us (2%)
    unnamed x6, waiting for transfers between devices  134 us
    dot_general x16, matrix products, term_step(): jnp.einsum('qp,spad->sqad', site_piece, applied, precision=lax.Precision....  59.3 us
    dot_general x16, matrix products, term_step(): jnp.einsum('sab,spbd->spad', left_piece, right_done, preferred_element_ty...  46.6 us
    dot_general x16, local copies, waits for them, and re-layouts, term_step(): jnp.einsum('sab,spbd->spad', left_piece, right_done, preferred_element_ty...  40.3 us
    all_gather x2, waiting for transfers between devices, apply_hamiltonian(): gathered = lax.all_gather(local_vec, 'ops', axis=1, tiled=True)  33.8 us
    psum x1, blocking collectives, body(): lax.psum((jnp.sum(wide_wave * wide_wave), jnp.sum(wide_wave * first_sigma...  31.7 us
    dynamic_update_slice x16, local copies, waits for them, and re-layouts, term_step(): lax.dynamic_update_index_in_dim(running, current + blended, bucket_slot, 0)  31.2 us
    psum x1, blocking collectives, body(): corr_norm = lax.psum(jnp.sum(correction * correction), ('bond', 'ops'))  30.1 us
  transfers between devices with their start and end apart: 8, of which 6 were waited for; matrix products, arithmetic and copies ran while one was open for 1% of the time, Pallas kernels for 0%

commit v1 on v0

v1 whole, which is shorter than its diff:
```python
import functools

import jax
import jax.numpy as jnp
from jax import lax
from jax.experimental import pallas as pl
from jax.experimental.pallas import tpu as pltpu
from jax.sharding import PartitionSpec as P

F32 = jnp.float32
BF16 = jnp.bfloat16
SUB = 16
CORES = 2
CHUNKS = 4


def kernel(
    n_ops,
    n_bond,
    left_len,
    right_len,
    wave,
    left,
    right,
    site,
    precond,
    out1,
    out2,
    vg,
    lg,
    rg,
    sg,
    mixed,
    xs,
    acc,
    bsend,
    brecv,
    red,
    v_sems,
    vf_sems,
    lr_sib,
    lr_x,
    lr_f,
    site_sems,
    bond_sems,
    red_sems,
):
    terms, sectors, width, _ = left.shape
    mine = wave.shape[1]
    states = vg.shape[1]
    n_x = n_ops // CORES
    per = terms // CHUNKS
    me = lax.axis_index("ops")
    bond = lax.axis_index("bond")
    core = lax.rem(me, CORES)
    chip = me // CORES
    sibling = me + 1 - 2 * core

    def ops_at(offset):
        return lax.rem(me + offset, n_ops)

    def bond_at(offset):
        return lax.rem(bond + offset, n_bond)

    def same_core(offset):
        return lax.rem(chip + offset, n_x) * CORES + core

    def remote(src, dst, sems, target):
        return pltpu.make_async_remote_copy(
            src_ref=src,
            dst_ref=dst,
            send_sem=sems[0],
            recv_sem=sems[1],
            device_id=target,
            device_id_type=pl.DeviceIdType.MESH,
        )

    brecv[...] = jnp.zeros_like(brecv)
    barrier = pltpu.get_barrier_semaphore()
    for j in range(1, n_ops):
        pl.semaphore_signal(barrier, inc=1, device_id={"ops": ops_at(j)}, device_id_type=pl.DeviceIdType.MESH)
    for j in range(1, n_bond):
        pl.semaphore_signal(barrier, inc=1, device_id={"bond": bond_at(j)}, device_id_type=pl.DeviceIdType.MESH)

    rows_at = lax.broadcasted_iota(jnp.int32, (width, width), 0)
    cols_at = lax.broadcasted_iota(jnp.int32, (width, width), 1)

    def valid(s):
        keep = (rows_at < left_len[s]) & (cols_at < right_len[s])
        return jnp.where(keep, 1.0, 0.0).astype(F32)

    own = pl.ds(me * mine, mine)
    norm_part = jnp.zeros((8, width), F32)
    for s in range(sectors):
        keep = valid(s)
        for q in range(mine):
            block = wave[s, q].astype(F32) * keep
            vg[0, me * mine + q, :, s * width : (s + 1) * width] = block.astype(BF16)
            norm_part += jnp.sum((block * block).reshape(width // 8, 8, width), axis=0)
    lg[0] = left[...]
    rg[0] = right[...]
    sg[0] = site[me]

    pl.semaphore_wait(barrier, n_ops - 1 + n_bond - 1)

    def v_copy(turn, offset):
        target = sibling if offset == 0 else same_core(offset)
        where = vg.at[turn, own]
        return remote(
            where, where, (v_sems.at[turn, offset, 0], v_sems.at[turn, offset, 1]), {"ops": target}
        )

    def v_forward(turn, offset):
        owner = same_core(n_x - offset)
        where = vg.at[turn, pl.ds(owner * mine, mine)]
        return remote(
            where, where, (vf_sems.at[turn, offset, 0], vf_sems.at[turn, offset, 1]), {"ops": sibling}
        )

    def start_v(turn):
        for j in range(1, n_x):
            v_copy(turn, j).start()
        v_copy(turn, 0).start()

    def finish_v(turn):
        for j in range(1, n_x):
            v_copy(turn, j).wait_recv()
            v_forward(turn, j).start()
        v_copy(turn, 0).wait_recv()
        for j in range(1, n_x):
            v_forward(turn, j).wait_recv()

    def drain_v(turn):
        for j in range(n_x):
            v_copy(turn, j).wait_send()
        for j in range(1, n_x):
            v_forward(turn, j).wait_send()

    def site_copy(j):
        return remote(
            site.at[ops_at(j)], sg.at[slot_at(j)], (site_sems.at[j, 0], site_sems.at[j, 1]), {"ops": ops_at(j)}
        )

    def slot_at(j):
        there = ops_at(j)
        step = lax.rem(there // CORES - chip + n_x, n_x)
        other = jnp.where(lax.rem(there, CORES) == core, 0, 1)
        return step * CORES + other

    def sib_copy(i):
        src, dst = ((right, rg), (left, lg))[i]
        return remote(src, dst.at[1], (lr_sib.at[i, 0], lr_sib.at[i, 1]), {"ops": sibling})

    def x_copy(offset, chunk, i):
        src, dst = ((right, rg), (left, lg))[i]
        part = pl.ds(chunk * per, per)
        return remote(
            src.at[part],
            dst.at[offset * CORES, part],
            (lr_x.at[offset, chunk, i, 0], lr_x.at[offset, chunk, i, 1]),
            {"ops": same_core(offset)},
        )

    def x_forward(offset, chunk, i):
        dst = (rg, lg)[i]
        part = pl.ds(chunk * per, per)
        return remote(
            dst.at[offset * CORES, part],
            dst.at[offset * CORES + 1, part],
            (lr_f.at[offset, chunk, i, 0], lr_f.at[offset, chunk, i, 1]),
            {"ops": sibling},
        )

    start_v(0)
    for j in range(1, n_ops):
        site_copy(j).start()
    for i in range(2):
        sib_copy(i).start()
    for offset in range(1, n_x):
        for chunk in range(CHUNKS):
            for i in range(2):
                x_copy(offset, chunk, i).start()

    lane = lax.broadcasted_iota(jnp.int32, (SUB, states * SUB), 1)
    sub = lax.broadcasted_iota(jnp.int32, (SUB, states * SUB), 0)
    eye = jnp.where((lane & (SUB - 1)) == sub, 1.0, 0.0).astype(F32)
    count = terms * mine

    def group(turn, slot):
        spread = (sg[slot, :count, :][:, None, :] * eye[None]).astype(BF16)
        spread = spread.reshape(count * SUB, states * SUB)
        for c in range(width // SUB):
            piece = vg[turn, :, c * SUB : (c + 1) * SUB, :].reshape(states * SUB, sectors * width)
            done = jnp.dot(spread, piece, preferred_element_type=F32)
            mixed[:, c * SUB : (c + 1) * SUB, :] = done.astype(BF16).reshape(count, SUB, sectors * width)
        blank = jnp.zeros((width, width), BF16)
        for k in range(terms):
            wide = jnp.concatenate(
                [
                    jnp.concatenate([rg[slot, k, s] if s == u else blank for u in range(sectors)], axis=1)
                    for s in range(sectors)
                ],
                axis=0,
            )
            rows = mixed[k * mine : (k + 1) * mine].reshape(mine * width, sectors * width)
            done = lax.dot_general(
                rows, wide, (((1,), (1,)), ((), ())), preferred_element_type=F32
            ).astype(BF16)
            for q in range(mine):
                for s in range(sectors):
                    xs[s, k * width : (k + 1) * width, q * width : (q + 1) * width] = done[
                        q * width : (q + 1) * width, s * width : (s + 1) * width
                    ]
        for s in range(sectors):
            tall = []
            for d in range(3):
                pieces = []
                for k in range(terms):
                    at = count + d * terms + k
                    flag = sg[slot, at : at + 1, :width].astype(BF16)
                    pieces.append(lg[slot, k, s] * flag)
                tall.append(jnp.concatenate(pieces, axis=1))
            acc[s] += jnp.dot(jnp.concatenate(tall, axis=0), xs[s], preferred_element_type=F32)

    def bond_copy(turn, way):
        target = bond + 1 if way == 0 else bond - 1
        return remote(
            bsend.at[turn, way],
            brecv.at[turn, way],
            (bond_sems.at[turn, way, 0], bond_sems.at[turn, way, 1]),
            {"bond": target},
        )

    last = sectors - 1
    has_next = bond < n_bond - 1
    has_prev = bond > 0

    def exchange(turn):
        bsend[turn, 0] = acc[last, 2 * width :, :].astype(BF16)
        bsend[turn, 1] = acc[0, :width, :].astype(BF16)

        @pl.when(has_next)
        def _():
            bond_copy(turn, 0).start()

        @pl.when(has_prev)
        def _():
            bond_copy(turn, 1).start()

        @pl.when(has_prev)
        def _():
            bond_copy(turn, 0).wait_recv()

        @pl.when(has_next)
        def _():
            bond_copy(turn, 1).wait_recv()

        @pl.when(has_next)
        def _():
            bond_copy(turn, 0).wait_send()

        @pl.when(has_prev)
        def _():
            bond_copy(turn, 1).wait_send()

    def sigma(turn, s, q):
        cols = slice(q * width, (q + 1) * width)
        total = acc[s, width : 2 * width, cols]
        if s > 0:
            total += acc[s - 1, 2 * width :, cols]
        else:
            total += brecv[turn, 0, :, cols].astype(F32)
        if s < last:
            total += acc[s + 1, :width, cols]
        else:
            total += brecv[turn, 1, :, cols].astype(F32)
        return total * valid(s)

    def red_copy(turn, stage, j):
        target = {"ops": ops_at(j)} if stage == 0 else {"bond": bond_at(j)}
        return remote(
            red.at[turn, stage, 0],
            red.at[turn, stage, j],
            (red_sems.at[turn, stage, j, 0], red_sems.at[turn, stage, j, 1]),
            target,
        )

    def red_start(turn, stage, value):
        red[turn, stage, 0] = value
        for j in range(1, (n_ops, n_bond)[stage]):
            red_copy(turn, stage, j).start()

    def red_finish(turn, stage):
        size = (n_ops, n_bond)[stage]
        for j in range(1, size):
            red_copy(turn, stage, j).wait_recv()
        for j in range(1, size):
            red_copy(turn, stage, j).wait_send()
        total = red[turn, stage, 0]
        for j in range(1, size):
            total += red[turn, stage, j]
        return total

    acc[...] = jnp.zeros_like(acc)
    finish_v(0)
    for j in range(1, n_ops):
        site_copy(j).wait_recv()

    def step(slot, carry):
        @pl.when(slot == 1)
        def _():
            for i in range(2):
                sib_copy(i).wait_recv()

        @pl.when((slot >= CORES) & (lax.rem(slot, CORES) == 0))
        def _():
            offset = slot // CORES
            for chunk in range(CHUNKS):
                for i in range(2):
                    x_copy(offset, chunk, i).wait_recv()
                    x_forward(offset, chunk, i).start()

        @pl.when((slot >= CORES) & (lax.rem(slot, CORES) == 1))
        def _():
            offset = slot // CORES
            for chunk in range(CHUNKS):
                for i in range(2):
                    x_forward(offset, chunk, i).wait_recv()

        group(0, slot)
        return carry

    lax.fori_loop(0, n_ops, step, 0)
    exchange(0)
    sig_part = jnp.zeros((8, width), F32)
    for s in range(sectors):
        for q in range(mine):
            block = sigma(0, s, q)
            out1[s, q] = block
            start = vg[0, me * mine + q, :, s * width : (s + 1) * width].astype(F32)
            sig_part += jnp.sum((block * start).reshape(width // 8, 8, width), axis=0)
    red_start(0, 0, jnp.concatenate([norm_part, sig_part], axis=0))
    red_start(0, 1, red_finish(0, 0))
    total = red_finish(0, 1)
    wave_norm = jnp.sum(total[:8])
    ritz = jnp.sum(total[8:]) / wave_norm
    corr_part = jnp.zeros((8, width), F32)
    for s in range(sectors):
        for q in range(mine):
            start = vg[0, me * mine + q, :, s * width : (s + 1) * width].astype(F32)
            corr = (out1[s, q] - ritz * start) / precond[s, q]
            vg[1, me * mine + q, :, s * width : (s + 1) * width] = corr.astype(BF16)
            corr_part += jnp.sum((corr * corr).reshape(width // 8, 8, width), axis=0)
    start_v(1)
    red_start(1, 0, jnp.concatenate([corr_part, corr_part], axis=0))
    acc[...] = jnp.zeros_like(acc)
    finish_v(1)
    red_start(1, 1, red_finish(1, 0))

    def again(slot, carry):
        group(1, slot)
        return carry

    lax.fori_loop(0, n_ops, again, 0)
    corr_norm = jnp.sum(red_finish(1, 1)[:8])
    scale = jnp.sqrt(jnp.full((1, width), wave_norm / (corr_norm + 1e-06), F32))
    exchange(1)
    for s in range(sectors):
        for q in range(mine):
            out2[s, q] = sigma(1, s, q) * scale

    drain_v(0)
    drain_v(1)
    for j in range(1, n_ops):
        site_copy(j).wait_send()
    for i in range(2):
        sib_copy(i).wait_send()
    for offset in range(1, n_x):
        for chunk in range(CHUNKS):
            for i in range(2):
                x_copy(offset, chunk, i).wait_send()
                x_forward(offset, chunk, i).wait_send()


def body(
    n_ops,
    n_bond,
    wavefunction,
    left_blocks,
    right_blocks,
    site_blocks,
    preconditioner,
    left_lengths,
    right_lengths,
    term_shift,
):
    sectors, mine, width, _ = wavefunction.shape
    terms = left_blocks.shape[0]
    states = site_blocks.shape[1]
    lanes = states * SUB
    spread = site_blocks.reshape(terms, n_ops, mine, states).transpose(1, 0, 2, 3)
    spread = jnp.repeat(spread.reshape(n_ops, terms * mine, states), SUB, axis=2)
    flags = (term_shift[None, :] == jnp.arange(-1, 2, dtype=jnp.int32)[:, None]).astype(F32)
    flags = jnp.broadcast_to(flags.reshape(1, 3 * terms, 1), (n_ops, 3 * terms, lanes))
    site = jnp.concatenate([spread, flags], axis=1)
    rows = site.shape[1]
    out = jax.ShapeDtypeStruct((sectors, mine, width, width), F32)
    vmem = pl.BlockSpec(memory_space=pltpu.VMEM)
    smem = pl.BlockSpec(memory_space=pltpu.SMEM)
    n_x = n_ops // CORES
    most = max(n_ops, n_bond)
    dma = pltpu.SemaphoreType.DMA
    first, second = pl.pallas_call(
        functools.partial(kernel, n_ops, n_bond),
        out_shape=(out, out),
        in_specs=[smem, smem] + [vmem] * 5,
        out_specs=(vmem, vmem),
        scratch_shapes=[
            pltpu.VMEM((2, states, width, sectors * width), BF16),
            pltpu.VMEM((n_ops, terms, sectors, width, width), BF16),
            pltpu.VMEM((n_ops, terms, sectors, width, width), BF16),
            pltpu.VMEM((n_ops, rows, lanes), F32),
            pltpu.VMEM((terms * mine, width, sectors * width), BF16),
            pltpu.VMEM((sectors, terms * width, mine * width), BF16),
            pltpu.VMEM((sectors, 3 * width, mine * width), F32),
            pltpu.VMEM((2, 2, width, mine * width), BF16),
            pltpu.VMEM((2, 2, width, mine * width), BF16),
            pltpu.VMEM((2, 2, most, 16, width), F32),
            dma((2, n_x, 2)),
            dma((2, n_x, 2)),
            dma((2, 2)),
            dma((n_x, CHUNKS, 2, 2)),
            dma((n_x, CHUNKS, 2, 2)),
            dma((n_ops, 2)),
            dma((2, 2, 2)),
            dma((2, 2, most, 2)),
        ],
        compiler_params=pltpu.CompilerParams(
            collective_id=0, has_side_effects=True, vmem_limit_bytes=48 * 1024 * 1024
        ),
    )(left_lengths, right_lengths, wavefunction, left_blocks, right_blocks, site, preconditioner)
    return first, second


def solution(mesh):
    in_specs = (
        P(("grp", "bond"), "ops", None, None),
        P(("grp", "ops"), "bond", None, None),
        P(("grp", "ops"), "bond", None, None),
        P(("grp", "ops"), None, None),
        P(("grp", "bond"), "ops", None, None),
        P(("grp", "bond")),
        P(("grp", "bond")),
        P(("grp", "ops")),
    )
    out_specs = (P(("grp", "bond"), "ops", None, None), P(("grp", "bond"), "ops", None, None))
    run = functools.partial(body, mesh.shape["ops"], mesh.shape["bond"])
    return jax.shard_map(run, mesh=mesh, in_specs=in_specs, out_specs=out_specs, check_vma=False)
```

time: 552 us -> 80.1 us (0.15); the launches traced: 546 us -> 79.9 us
  waiting for transfers between devices: 172 us -> 0 us
  matrix products: 126 us -> 0 us
  local copies, waits for them, and re-layouts: 119 us -> 5.52 us
  Pallas kernels: 0 us -> 73.5 us
  blocking collectives: 61.8 us -> 0 us
  loops' own time: 21.3 us -> 0 us
  other arithmetic: 19 us -> 0.16 us
  between operations: 17.1 us -> 0.7 us
  starting transfers between devices: 10.2 us -> 0 us
    unnamed x6 -> x0, waiting for transfers between devices: 134 us -> none
    dot_general x48 -> x0, matrix products: 126 us -> none  [the longest x16 59.3 us: term_step(): jnp.einsum('qp,spad->sqad', site_piece, applied, precision=lax.Precision....]
    pallas_call x0 -> x1, Pallas kernels: none -> 73.5 us  [body(): pl.pallas_call(functools.partial(kernel, n_ops, n_bond), out_shape=(out,...]
    psum x2 -> x0, blocking collectives: 61.8 us -> none  [the longest x1 31.7 us: body(): lax.psum((jnp.sum(wide_wave * wide_wave), jnp.sum(wide_wave * first_sigma...]
    dot_general x16 -> x0, local copies, waits for them, and re-layouts: 40.3 us -> none  [term_step(): jnp.einsum('sab,spbd->spad', left_piece, right_done, preferred_element_ty...]
    dynamic_slice x32 -> x0, local copies, waits for them, and re-layouts: 37.1 us -> none  [the longest x16 27.8 us: term_step(): current = lax.dynamic_index_in_dim(running, bucket_slot, 0, keepdims=False)]
    all_gather x2 -> x0, waiting for transfers between devices: 33.8 us -> none  [apply_hamiltonian(): gathered = lax.all_gather(local_vec, 'ops', axis=1, tiled=True)]
    dynamic_update_slice x16 -> x0, local copies, waits for them, and re-layouts: 31.2 us -> none  [term_step(): lax.dynamic_update_index_in_dim(running, current + blended, bucket_slot, 0)]
  transfers between devices with their start and end apart: 8 -> 0, of which waited for: 6 -> 0; matrix products, arithmetic and copies ran while one was open for 1% -> 0% of each run, Pallas kernels for 0% -> 0%
where the time goes in v1:
time: 80.1 us; the launch traced here: 79.9 us
  Pallas kernels  73.5 us (92%)
  local copies, waits for them, and re-layouts  5.52 us (7%)
    pallas_call x1, Pallas kernels, body(): pl.pallas_call(functools.partial(kernel, n_ops, n_bond), out_shape=(out,...  73.5 us
    unnamed x16, local copies, waits for them, and re-layouts  4.23 us

profile of v1, /device:TPU:1, one launch (start us, length us, event | category | flops | bytes accessed | tf_op | source)
XLA Modules:
  0.0 79.9 jit_solution(10777059142187067847)
XLA Ops:
  0.6 0.0 copy-start.6
  0.6 0.6 copy-done.6
  1.3 0.1 compare_convert_fusion
  1.4 0.1 reshape.40
  1.4 0.1 pad.1.clone
  1.5 0.9 %copy.10 = f32[8,4,4,16]{3,2,0,1:T(4,128)S(1)} copy(f32[8,4,4,16]{3,2,1,0:T(4,128)} %bitcast.7) | data formatting | bytes 16384 | tf_op jit(solution)/shard_map/reshape | solution.py:401
  2.4 0.1 copy.11
  2.5 0.0 copy-start.1
  2.5 0.0 copy-start.2
  2.5 0.0 copy-start
  2.5 0.2 copy.12
  2.7 0.0 copy-start.4
  2.7 0.0 copy-start.5
  2.7 0.1 pad_maximum_fusion.site
  2.8 0.7 copy-done.1
  3.5 0.2 copy-done.2
  3.7 0.2 copy-done
  3.8 0.0 copy-done.4
  3.8 0.0 copy-done.5
  3.8 0.0 copy-start.3
  3.8 0.9 %copy-done.3 = bf16[2,4,128,128]{3,2,1,0:T(8,128)(2,1)S(1)} copy-done((bf16[2,4,128,128]{3,2,1,0:T(8,128)(2,1)S(1)}, bf16[2,4,128,128]{3,2,1,0:T(8,128)(2,1)}, u32[]{:S(2)}) %copy-start.3) | copy-done | bytes 262168
  4.8 73.5 %shard_map.95 = (f32[2,4,128,128]{3,2,1,0:T(8,128)S(1)}, f32[2,4,128,128]{3,2,1,0:T(8,128)S(1)}) custom-call(s32[2]{0:T(128)S(1)} %copy-done.4, s32[2]{0:T(128)S(1)} %copy-done.5, bf16[2,4,128,128]{3,2,1,0:T(8,128)(2,1)S(1)} %copy-done.3, bf16[8,2,128,128]{3,2,1,0:T(8,128)(2,1)S(1)} %copy-done, bf16[8,2,128,128]{3,2,1,0:T(8,128)(2,1)S(1)} %copy-done.1, ...), custom_call_target="tpu_custom_call" | custom-call | tf_op jit(solution)/shard_map/pallas_call | solution.py:413
  78.3 0.8 copy.15
  79.1 0.8 copy.16
  (2 shorter events, 0.0 us)
Async XLA Ops:
  0.6 0.7 copy-start.6
  2.5 1.0 %copy-start.1 = (bf16[8,2,128,128]{3,2,1,0:T(8,128)(2,1)S(1)}, bf16[8,2,128,128]{3,2,1,0:T(8,128)(2,1)}, u32[]{:S(2)}) copy-start(bf16[8,2,128,128]{3,2,1,0:T(8,128)(2,1)} %right.1) | copy-start | bytes 1572868
  2.5 1.2 %copy-start.2 = (f32[2,4,128,128]{3,2,1,0:T(8,128)S(1)}, f32[2,4,128,128]{3,2,1,0:T(8,128)}, u32[]{:S(2)}) copy-start(f32[2,4,128,128]{3,2,1,0:T(8,128)} %precond.1) | copy-start | bytes 1572868
  2.5 1.3 %copy-start = (bf16[8,2,128,128]{3,2,1,0:T(8,128)(2,1)S(1)}, bf16[8,2,128,128]{3,2,1,0:T(8,128)(2,1)}, u32[]{:S(2)}) copy-start(bf16[8,2,128,128]{3,2,1,0:T(8,128)(2,1)} %left.1) | copy-start | bytes 1572868
  2.7 1.1 %copy-start.4 = (s32[2]{0:T(128)S(1)}, s32[2]{0:T(128)}, u32[]{:S(2)}) copy-start(s32[2]{0:T(128)} %left_len.1) | copy-start | bytes 28
  2.7 1.1 %copy-start.5 = (s32[2]{0:T(128)S(1)}, s32[2]{0:T(128)}, u32[]{:S(2)}) copy-start(s32[2]{0:T(128)} %right_len.1) | copy-start | bytes 28
  3.8 1.0 %copy-start.3 = (bf16[2,4,128,128]{3,2,1,0:T(8,128)(2,1)S(1)}, bf16[2,4,128,128]{3,2,1,0:T(8,128)(2,1)}, u32[]{:S(2)}) copy-start(bf16[2,4,128,128]{3,2,1,0:T(8,128)(2,1)} %wave.1) | copy-start | bytes 786436

commit v2 on v1

--- a/solution.py
+++ b/solution.py
@@ -12,6 +12,7 @@
 SUB = 16
 CORES = 2
 CHUNKS = 4
+FLAT = 0
 
 
 def kernel(
@@ -35,6 +36,8 @@
     acc,
     bsend,
     brecv,
+    edge,
+    pre,
     red,
     v_sems,
     vf_sems,
@@ -44,6 +47,8 @@
     site_sems,
     bond_sems,
     red_sems,
+    edge_sems,
+    own_sems,
 ):
     terms, sectors, width, _ = left.shape
     mine = wave.shape[1]
@@ -59,6 +64,13 @@
     def ops_at(offset):
         return lax.rem(me + offset, n_ops)
 
+    everyone = n_ops * n_bond
+    flat = everyone <= FLAT
+
+    def all_at(offset):
+        there = lax.rem(bond * n_ops + me + offset, everyone)
+        return {"bond": there // n_ops, "ops": lax.rem(there, n_ops)}
+
     def bond_at(offset):
         return lax.rem(bond + offset, n_bond)
 
@@ -76,11 +88,22 @@
         )
 
     brecv[...] = jnp.zeros_like(brecv)
+    edge[...] = jnp.zeros_like(edge)
     barrier = pltpu.get_barrier_semaphore()
-    for j in range(1, n_ops):
-        pl.semaphore_signal(barrier, inc=1, device_id={"ops": ops_at(j)}, device_id_type=pl.DeviceIdType.MESH)
-    for j in range(1, n_bond):
-        pl.semaphore_signal(barrier, inc=1, device_id={"bond": bond_at(j)}, device_id_type=pl.DeviceIdType.MESH)
+    if flat:
+        for j in range(1, everyone):
+            pl.semaphore_signal(barrier, inc=1, device_id=all_at(j), device_id_type=pl.DeviceIdType.MESH)
+    else:
+        for j in range(1, n_ops):
+            pl.semaphore_signal(barrier, inc=1, device_id={"ops": ops_at(j)}, device_id_type=pl.DeviceIdType.MESH)
+        for j in range(1, n_bond):
+            pl.semaphore_signal(barrier, inc=1, device_id={"bond": bond_at(j)}, device_id_type=pl.DeviceIdType.MESH)
+    fetches = [
+        pltpu.make_async_copy(src, dst, own_sems.at[i])
+        for i, (src, dst) in enumerate(((right, rg.at[0]), (left, lg.at[0]), (precond, pre)))
+    ]
+    for fetch in fetches:
+        fetch.start()
 
     rows_at = lax.broadcasted_iota(jnp.int32, (width, width), 0)
     cols_at = lax.broadcasted_iota(jnp.int32, (width, width), 1)
@@ -97,11 +120,9 @@
             block = wave[s, q].astype(F32) * keep
             vg[0, me * mine + q, :, s * width : (s + 1) * width] = block.astype(BF16)
             norm_part += jnp.sum((block * block).reshape(width // 8, 8, width), axis=0)
-    lg[0] = left[...]
-    rg[0] = right[...]
     sg[0] = site[me]
 
-    pl.semaphore_wait(barrier, n_ops - 1 + n_bond - 1)
+    pl.semaphore_wait(barrier, everyone - 1 if flat else n_ops - 1 + n_bond - 1)
 
     def v_copy(turn, offset):
         target = sibling if offset == 0 else same_core(offset)
@@ -171,7 +192,29 @@
             {"ops": sibling},
         )
 
+    last = sectors - 1
+    has_next = bond < n_bond - 1
+    has_prev = bond > 0
+
+    def edge_copy(way):
+        at = 0 if way == 0 else last
+        return remote(
+            vg.at[0, own, :, pl.ds(at * width, width)],
+            edge.at[way],
+            (edge_sems.at[way, 0], edge_sems.at[way, 1]),
+            {"bond": bond - 1 if way == 0 else bond + 1},
+        )
+
     start_v(0)
+
+    @pl.when(has_prev)
+    def _():
+        edge_copy(0).start()
+
+    @pl.when(has_next)
+    def _():
+        edge_copy(1).start()
+
     for j in range(1, n_ops):
         site_copy(j).start()
     for i in range(2):
@@ -186,18 +229,21 @@
     eye = jnp.where((lane & (SUB - 1)) == sub, 1.0, 0.0).astype(F32)
     count = terms * mine
 
-    def group(turn, slot):
-        spread = (sg[slot, :count, :][:, None, :] * eye[None]).astype(BF16)
-        spread = spread.reshape(count * SUB, states * SUB)
+    def group(turn, slot, first, size):
+        rows_in = size * mine
+        spread = (sg[slot, first * mine : first * mine + rows_in, :][:, None, :] * eye[None]).astype(BF16)
+        spread = spread.reshape(rows_in * SUB, states * SUB)
         for c in range(width // SUB):
             piece = vg[turn, :, c * SUB : (c + 1) * SUB, :].reshape(states * SUB, sectors * width)
             done = jnp.dot(spread, piece, preferred_element_type=F32)
-            mixed[:, c * SUB : (c + 1) * SUB, :] = done.astype(BF16).reshape(count, SUB, sectors * width)
+            mixed[:rows_in, c * SUB : (c + 1) * SUB, :] = done.astype(BF16).reshape(
+                rows_in, SUB, sectors * width
+            )
         blank = jnp.zeros((width, width), BF16)
-        for k in range(terms):
+        for k in range(size):
             wide = jnp.concatenate(
                 [
-                    jnp.concatenate([rg[slot, k, s] if s == u else blank for u in range(sectors)], axis=1)
+                    jnp.concatenate([rg[slot, first + k, s] if s == u else blank for u in range(sectors)], axis=1)
                     for s in range(sectors)
                 ],
                 axis=0,
@@ -215,12 +261,14 @@
             tall = []
             for d in range(3):
                 pieces = []
-                for k in range(terms):
-                    at = count + d * terms + k
+                for k in range(size):
+                    at = count + d * terms + first + k
                     flag = sg[slot, at : at + 1, :width].astype(BF16)
-                    pieces.append(lg[slot, k, s] * flag)
+                    pieces.append(lg[slot, first + k, s] * flag)
                 tall.append(jnp.concatenate(pieces, axis=1))
-            acc[s] += jnp.dot(jnp.concatenate(tall, axis=0), xs[s], preferred_element_type=F32)
+            acc[s] += jnp.dot(
+                jnp.concatenate(tall, axis=0), xs[s, : size * width], preferred_element_type=F32
+            )
 
     def bond_copy(turn, way):
         target = bond + 1 if way == 0 else bond - 1
@@ -231,11 +279,7 @@
             {"bond": target},
         )
 
-    last = sectors - 1
-    has_next = bond < n_bond - 1
-    has_prev = bond > 0
-
-    def exchange(turn):
+    def exchange_start(turn):
         bsend[turn, 0] = acc[last, 2 * width :, :].astype(BF16)
         bsend[turn, 1] = acc[0, :width, :].astype(BF16)
 
@@ -247,6 +291,7 @@
         def _():
             bond_copy(turn, 1).start()
 
+    def exchange_finish(turn):
         @pl.when(has_prev)
         def _():
             bond_copy(turn, 0).wait_recv()
@@ -263,21 +308,28 @@
         def _():
             bond_copy(turn, 1).wait_send()
 
-    def sigma(turn, s, q):
-        cols = slice(q * width, (q + 1) * width)
+    def near_sum(s, cols):
         total = acc[s, width : 2 * width, cols]
         if s > 0:
             total += acc[s - 1, 2 * width :, cols]
-        else:
-            total += brecv[turn, 0, :, cols].astype(F32)
         if s < last:
             total += acc[s + 1, :width, cols]
-        else:
+        return total
+
+    def sigma(turn, s, q):
+        cols = slice(q * width, (q + 1) * width)
+        total = near_sum(s, cols)
+        if s == 0:
+            total += brecv[turn, 0, :, cols].astype(F32)
+        if s == last:
             total += brecv[turn, 1, :, cols].astype(F32)
         return total * valid(s)
 
     def red_copy(turn, stage, j):
-        target = {"ops": ops_at(j)} if stage == 0 else {"bond": bond_at(j)}
+        if flat:
+            target = all_at(j)
+        else:
+            target = {"ops": ops_at(j)} if stage == 0 else {"bond": bond_at(j)}
         return remote(
             red.at[turn, stage, 0],
             red.at[turn, stage, j],
@@ -287,11 +339,11 @@
 
     def red_start(turn, stage, value):
         red[turn, stage, 0] = value
-        for j in range(1, (n_ops, n_bond)[stage]):
+        for j in range(1, everyone if flat else (n_ops, n_bond)[stage]):
             red_copy(turn, stage, j).start()
 
     def red_finish(turn, stage):
-        size = (n_ops, n_bond)[stage]
+        size = everyone if flat else (n_ops, n_bond)[stage]
         for j in range(1, size):
             red_copy(turn, stage, j).wait_recv()
         for j in range(1, size):
@@ -306,68 +358,100 @@
     for j in range(1, n_ops):
         site_copy(j).wait_recv()
 
-    def step(slot, carry):
+    fetches[0].wait()
+    fetches[1].wait()
+
+    def near(slot, carry):
         @pl.when(slot == 1)
         def _():
             for i in range(2):
                 sib_copy(i).wait_recv()
 
-        @pl.when((slot >= CORES) & (lax.rem(slot, CORES) == 0))
-        def _():
-            offset = slot // CORES
-            for chunk in range(CHUNKS):
-                for i in range(2):
-                    x_copy(offset, chunk, i).wait_recv()
-                    x_forward(offset, chunk, i).start()
-
-        @pl.when((slot >= CORES) & (lax.rem(slot, CORES) == 1))
-        def _():
-            offset = slot // CORES
-            for chunk in range(CHUNKS):
-                for i in range(2):
-                    x_forward(offset, chunk, i).wait_recv()
-
-        group(0, slot)
+        group(0, slot, 0, terms)
         return carry
 
-    lax.fori_loop(0, n_ops, step, 0)
-    exchange(0)
+    def step(offset, carry):
+        for chunk in range(CHUNKS):
+            for i in range(2):
+                x_copy(offset, chunk, i).wait_recv()
+                x_forward(offset, chunk, i).start()
+            group(0, offset * CORES, chunk * per, per)
+            for i in range(2):
+                x_forward(offset, chunk, i).wait_recv()
+            group(0, offset * CORES + 1, chunk * per, per)
+        return carry
+
+    lax.fori_loop(0, CORES, near, 0)
+    lax.fori_loop(1, n_x, step, 0)
+    exchange_start(0)
+    fetches[2].wait()
+
+    @pl.when(has_next)
+    def _():
+        edge_copy(0).wait_recv()
+
+    @pl.when(has_prev)
+    def _():
+        edge_copy(1).wait_recv()
+
+    def fold(block):
+        return jnp.sum(block.reshape(width // 8, 8, width), axis=0)
+
     sig_part = jnp.zeros((8, width), F32)
+    for q in range(mine):
+        cols = slice(q * width, (q + 1) * width)
+        for way in range(2):
+            sig_part += fold(bsend[0, way, :, cols].astype(F32) * edge[way, q].astype(F32))
+        for s in range(sectors):
+            start = vg[0, me * mine + q, :, s * width : (s + 1) * width].astype(F32)
+            sig_part += fold(near_sum(s, cols) * start)
+    red_start(0, 0, jnp.concatenate([norm_part, sig_part], axis=0))
+    if flat:
+        total = red_finish(0, 0)
+    else:
+        red_start(0, 1, red_finish(0, 0))
+        total = red_finish(0, 1)
+    exchange_finish(0)
     for s in range(sectors):
         for q in range(mine):
-            block = sigma(0, s, q)
-            out1[s, q] = block
-            start = vg[0, me * mine + q, :, s * width : (s + 1) * width].astype(F32)
-            sig_part += jnp.sum((block * start).reshape(width // 8, 8, width), axis=0)
-    red_start(0, 0, jnp.concatenate([norm_part, sig_part], axis=0))
-    red_start(0, 1, red_finish(0, 0))
-    total = red_finish(0, 1)
+            out1[s, q] = sigma(0, s, q)
     wave_norm = jnp.sum(total[:8])
     ritz = jnp.sum(total[8:]) / wave_norm
     corr_part = jnp.zeros((8, width), F32)
     for s in range(sectors):
         for q in range(mine):
             start = vg[0, me * mine + q, :, s * width : (s + 1) * width].astype(F32)
-            corr = (out1[s, q] - ritz * start) / precond[s, q]
+            corr = (out1[s, q] - ritz * start) / pre[s, q]
             vg[1, me * mine + q, :, s * width : (s + 1) * width] = corr.astype(BF16)
             corr_part += jnp.sum((corr * corr).reshape(width // 8, 8, width), axis=0)
+    red_start(1, 0, jnp.concatenate([corr_part, corr_part], axis=0))
     start_v(1)
-    red_start(1, 0, jnp.concatenate([corr_part, corr_part], axis=0))
     acc[...] = jnp.zeros_like(acc)
     finish_v(1)
-    red_start(1, 1, red_finish(1, 0))
+    if not flat:
+        red_start(1, 1, red_finish(1, 0))
 
     def again(slot, carry):
-        group(1, slot)
+        group(1, slot, 0, terms)
         return carry
 
     lax.fori_loop(0, n_ops, again, 0)
-    corr_norm = jnp.sum(red_finish(1, 1)[:8])
+    exchange_start(1)
+    corr_norm = jnp.sum(red_finish(1, 0 if flat else 1)[:8])
     scale = jnp.sqrt(jnp.full((1, width), wave_norm / (corr_norm + 1e-06), F32))
-    exchange(1)
+    exchange_finish(1)
     for s in range(sectors):
         for q in range(mine):
             out2[s, q] = sigma(1, s, q) * scale
+
+
+    @pl.when(has_prev)
+    def _():
+        edge_copy(0).wait_send()
+
+    @pl.when(has_next)
+    def _():
+        edge_copy(1).wait_send()
 
     drain_v(0)
     drain_v(1)
@@ -406,14 +490,15 @@
     rows = site.shape[1]
     out = jax.ShapeDtypeStruct((sectors, mine, width, width), F32)
     vmem = pl.BlockSpec(memory_space=pltpu.VMEM)
+    far = pl.BlockSpec(memory_space=pl.ANY)
     smem = pl.BlockSpec(memory_space=pltpu.SMEM)
     n_x = n_ops // CORES
-    most = max(n_ops, n_bond)
+    most = n_ops * n_bond if n_ops * n_bond <= FLAT else max(n_ops, n_bond)
     dma = pltpu.SemaphoreType.DMA
     first, second = pl.pallas_call(
         functools.partial(kernel, n_ops, n_bond),
         out_shape=(out, out),
-        in_specs=[smem, smem] + [vmem] * 5,
+        in_specs=[smem, smem, vmem, far, far, vmem, far],
         out_specs=(vmem, vmem),
         scratch_shapes=[
             pltpu.VMEM((2, states, width, sectors * width), BF16),
@@ -425,6 +510,8 @@
             pltpu.VMEM((sectors, 3 * width, mine * width), F32),
             pltpu.VMEM((2, 2, width, mine * width), BF16),
             pltpu.VMEM((2, 2, width, mine * width), BF16),
+            pltpu.VMEM((2, mine, width, width), BF16),
+            pltpu.VMEM((sectors, mine, width, width), F32),
             pltpu.VMEM((2, 2, most, 16, width), F32),
             dma((2, n_x, 2)),
             dma((2, n_x, 2)),
@@ -434,6 +521,8 @@
             dma((n_ops, 2)),
             dma((2, 2, 2)),
             dma((2, 2, most, 2)),
+            dma((2, 2)),
+            dma((3,)),
         ],
         compiler_params=pltpu.CompilerParams(
             collective_id=0, has_side_effects=True, vmem_limit_bytes=48 * 1024 * 1024

time: 80.1 us -> 74.3 us (0.928)
  Pallas kernels: 73.5 us -> 67.7 us
    pallas_call x1, Pallas kernels: 73.5 us -> 67.7 us  [body(): pl.pallas_call(functools.partial(kernel, n_ops, n_bond), out_shape=(out,...]
where the time goes in v2:
time: 74.3 us; the launch traced here: 74.1 us
  Pallas kernels  67.7 us (91%)
  local copies, waits for them, and re-layouts  5.52 us (7%)
    pallas_call x1, Pallas kernels, body(): pl.pallas_call(functools.partial(kernel, n_ops, n_bond), out_shape=(out,...  67.7 us
    unnamed x16, local copies, waits for them, and re-layouts  4.23 us

profile of v2, /device:TPU:1, one launch (start us, length us, event | category | flops | bytes accessed | tf_op | source)
XLA Modules:
  0.0 74.1 jit_solution(1021464800943968565)
XLA Ops:
  0.6 0.0 copy-start.6
  0.6 0.6 copy-done.6
  1.3 0.1 compare_convert_fusion
  1.4 0.1 reshape.40
  1.4 0.1 pad.1.clone
  1.5 0.9 %copy.10 = f32[8,4,4,16]{3,2,0,1:T(4,128)S(1)} copy(f32[8,4,4,16]{3,2,1,0:T(4,128)} %bitcast.7) | data formatting | bytes 16384 | tf_op jit(solution)/shard_map/reshape | solution.py:485
  2.4 0.1 copy.11
  2.5 0.0 copy-start.1
  2.5 0.0 copy-start.2
  2.5 0.0 copy-start
  2.5 0.2 copy.12
  2.7 0.0 copy-start.4
  2.7 0.0 copy-start.5
  2.7 0.1 pad_maximum_fusion.site
  2.8 0.7 copy-done.1
  3.5 0.2 copy-done.2
  3.7 0.2 copy-done
  3.8 0.0 copy-done.4
  3.8 0.0 copy-done.5
  3.8 0.0 copy-start.3
  3.8 0.9 %copy-done.3 = bf16[2,4,128,128]{3,2,1,0:T(8,128)(2,1)S(1)} copy-done((bf16[2,4,128,128]{3,2,1,0:T(8,128)(2,1)S(1)}, bf16[2,4,128,128]{3,2,1,0:T(8,128)(2,1)}, u32[]{:S(2)}) %copy-start.3) | copy-done | bytes 262168
  4.8 67.7 %shard_map.95 = (f32[2,4,128,128]{3,2,1,0:T(8,128)S(1)}, f32[2,4,128,128]{3,2,1,0:T(8,128)S(1)}) custom-call(s32[2]{0:T(128)S(1)} %copy-done.4, s32[2]{0:T(128)S(1)} %copy-done.5, bf16[2,4,128,128]{3,2,1,0:T(8,128)(2,1)S(1)} %copy-done.3, bf16[8,2,128,128]{3,2,1,0:T(8,128)(2,1)S(1)} %copy-done, bf16[8,2,128,128]{3,2,1,0:T(8,128)(2,1)S(1)} %copy-done.1, ...), custom_call_target="tpu_custom_call" | custom-call | tf_op jit(solution)/shard_map/pallas_call | solution.py:498
  72.5 0.8 %copy.15 = f32[2,4,128,128]{3,2,1,0:T(8,128)} copy(f32[2,4,128,128]{3,2,1,0:T(8,128)S(1)} %get-tuple-element.4) | data formatting | bytes 1048576
  73.3 0.8 %copy.16 = f32[2,4,128,128]{3,2,1,0:T(8,128)} copy(f32[2,4,128,128]{3,2,1,0:T(8,128)S(1)} %get-tuple-element.5) | data formatting | bytes 1048576
  (2 shorter events, 0.0 us)
Async XLA Ops:
  0.6 0.7 copy-start.6
  2.5 1.0 %copy-start.1 = (bf16[8,2,128,128]{3,2,1,0:T(8,128)(2,1)S(1)}, bf16[8,2,128,128]{3,2,1,0:T(8,128)(2,1)}, u32[]{:S(2)}) copy-start(bf16[8,2,128,128]{3,2,1,0:T(8,128)(2,1)} %right.1) | copy-start | bytes 1572868
  2.5 1.2 %copy-start.2 = (f32[2,4,128,128]{3,2,1,0:T(8,128)S(1)}, f32[2,4,128,128]{3,2,1,0:T(8,128)}, u32[]{:S(2)}) copy-start(f32[2,4,128,128]{3,2,1,0:T(8,128)} %precond.1) | copy-start | bytes 1572868
  2.5 1.3 %copy-start = (bf16[8,2,128,128]{3,2,1,0:T(8,128)(2,1)S(1)}, bf16[8,2,128,128]{3,2,1,0:T(8,128)(2,1)}, u32[]{:S(2)}) copy-start(bf16[8,2,128,128]{3,2,1,0:T(8,128)(2,1)} %left.1) | copy-start | bytes 1572868
  2.7 1.1 %copy-start.4 = (s32[2]{0:T(128)S(1)}, s32[2]{0:T(128)}, u32[]{:S(2)}) copy-start(s32[2]{0:T(128)} %left_len.1) | copy-start | bytes 28
  2.7 1.1 %copy-start.5 = (s32[2]{0:T(128)S(1)}, s32[2]{0:T(128)}, u32[]{:S(2)}) copy-start(s32[2]{0:T(128)} %right_len.1) | copy-start | bytes 28
  3.8 1.0 %copy-start.3 = (bf16[2,4,128,128]{3,2,1,0:T(8,128)(2,1)S(1)}, bf16[2,4,128,128]{3,2,1,0:T(8,128)(2,1)}, u32[]{:S(2)}) copy-start(bf16[2,4,128,128]{3,2,1,0:T(8,128)(2,1)} %wave.1) | copy-start | bytes 786436
